TPU v7x, 512 devices: a whole 4x4x16 slice. The times are simulated.
512 devices in a mesh: tm: 16 (over x, y_hi, core), height: 16 (over z), mp: 2 (over y_lo).
Axes of the slice: x: 4, y: 4 (y_hi: 2, y_lo: 2; y = y_hi * 2 + y_lo), z: 16, core: 2. Of those that a mesh axis runs over, the one named last changes fastest.
Arguments:
- queries: bfloat16 [16, 16, 384, 1536], P('tm', 'height', None, 'mp'), may hold values from -6 to 6
- key_field: bfloat16 [16, 16, 384, 1536], P('tm', 'height', None, 'mp'), may hold values from -10 to 10
- value_field: bfloat16 [16, 16, 384, 1536], P('tm', 'height', None, 'mp'), may hold values from -6 to 6
- stream: bfloat16 [16, 16, 384, 3072], P('tm', 'height', None, 'mp'), may hold values from -3 to 3
- gate_scale: float32 [3072], P('mp'), may hold values from 0.5 to 1.5
- out_weight: bfloat16 [1536, 3072], P('height', 'mp'), may hold values from -0.15625 to 0.15625
- tile_lists: int32 [16, 16, 9], P('tm', 'height'), may hold values from -1 to 255, as said below
Outputs:
- block_out: bfloat16 [16, 16, 384, 3072], P('tm', 'height', None, 'mp')
Inputs may be any that keep to these rules, and one draw needn't show every extreme that they name: `tile_lists`: entry e names tile (e // 16, e % 16). The list of tile (a, b) names distinct tiles in increasing order, followed by -1 entries; they are all tiles of a box whose first indices form a run within a - 1 to a + 1 inside the same video (same a // 16) and whose second indices form a run within b - 1 to b + 1 inside the same column tile (same b // 16), and the box holds tile (a, b). Some list names 9 tiles and some list holds -1.
All inputs are finite; a program needn't handle non-finite values.
Results may differ from a plain program's by a relative error of at most 0.0059.
Values may be sent and summed in bfloat16 or wider, within the bound.
A program may use at most 128 MiB of HBM per device.

v0:
```python
import math
import jax
import jax.numpy as jnp
from jax import lax
from jax.sharding import PartitionSpec as P

HD = 128


def with_halo(cells, sides, width):
    for axis, dim in sides:
        count = lax.axis_size(axis)
        ends = count - 1
        head = lax.slice_in_dim(cells, 0, width, axis=dim)
        tail = lax.slice_in_dim(cells, cells.shape[dim] - width, cells.shape[dim], axis=dim)
        cells = jnp.concatenate(
            [
                lax.ppermute(tail, axis, [(i, (i + 1) % count) for i in range(ends)]),
                cells,
                lax.ppermute(head, axis, [((i + 1) % count, i) for i in range(ends)]),
            ],
            axis=dim,
        )
    return cells


def slot_mask(tile_lists, frame_index, row_index, frame_count, row_count):
    offsets = jnp.arange(3, dtype=jnp.int32) - 1
    slot_frames = frame_index + offsets[:, None]
    slot_rows = row_index + offsets[None, :]
    slot_ids = slot_frames * row_count + slot_rows
    inside = (
        (slot_frames >= 0)
        & (slot_frames < frame_count)
        & (slot_rows >= 0)
        & (slot_rows < row_count)
    )
    listed = tile_lists.reshape(-1)
    named = jnp.any(slot_ids[:, :, None] == listed[None, None, :], axis=2)
    return named & inside


def dense_heads(query_rows, beside_all, chosen, head_count):
    tokens = query_rows.shape[0]
    key_rows = beside_all[0].reshape(9 * tokens, -1)
    value_rows = beside_all[1].reshape(9 * tokens, -1)
    key_bias = jnp.where(jnp.repeat(chosen.reshape(9), tokens), 0.0, -jnp.inf).astype(jnp.float32)
    score_scale = 1.0 / math.sqrt(HD)
    outputs = []
    for head_index in range(head_count):
        lower = head_index * HD
        upper = lower + HD
        scores = (
            lax.dot_general(
                query_rows[:, lower:upper],
                key_rows[:, lower:upper],
                (((1,), (1,)), ((), ())),
                preferred_element_type=jnp.float32,
            )
            * score_scale
            + key_bias[None, :]
        )
        row_max = jnp.max(scores, axis=1, keepdims=True)
        weights = jnp.exp(scores - row_max).astype(jnp.bfloat16)
        total = jnp.sum(weights.astype(jnp.float32), axis=1, keepdims=True)
        outputs.append(
            jnp.dot(weights, value_rows[:, lower:upper], preferred_element_type=jnp.float32) / total
        )
    return jnp.concatenate(outputs, axis=1).astype(jnp.bfloat16)


def local(queries, key_field, value_field, stream, gate_scale, out_weight, tile_lists):
    groups_here, strips_here, cells_here, channels = queries.shape
    tokens = groups_here * strips_here * cells_here
    head_count = channels // HD
    query_rows = queries.reshape(tokens, channels)
    paired = jnp.stack(
        [key_field.reshape(tokens, channels), value_field.reshape(tokens, channels)]
    ).reshape(2, 1, 1, tokens, channels)
    beside_all = with_halo(paired, (("tm", 1), ("height", 2)), 1)
    frame_index = lax.axis_index("tm")
    row_index = lax.axis_index("height")
    frame_count = lax.axis_size("tm")
    row_count = lax.axis_size("height")
    chosen = slot_mask(tile_lists, frame_index, row_index, frame_count, row_count)
    attended = dense_heads(query_rows, beside_all, chosen, head_count)
    gathered = lax.all_gather(attended, "mp", axis=1, tiled=True)
    full_weight = lax.all_gather(out_weight, "height", axis=0, tiled=True)
    mixed = jnp.dot(gathered, full_weight, preferred_element_type=jnp.float32)
    result = stream.reshape(tokens, -1).astype(jnp.float32) + gate_scale[None, :] * mixed
    return result.astype(jnp.bfloat16).reshape(stream.shape)


def solution(mesh):
    placed = (
        P("tm", "height", None, "mp"),
        P("tm", "height", None, "mp"),
        P("tm", "height", None, "mp"),
        P("tm", "height", None, "mp"),
        P("mp"),
        P("height", "mp"),
        P("tm", "height", None),
    )
    return jax.shard_map(
        local, mesh=mesh, in_specs=placed, out_specs=P("tm", "height", None, "mp"), check_vma=False
    )
```

profile of v0, /device:TPU:10, one launch (start us, length us, event | category | flops | bytes accessed | tf_op | source)
XLA Modules:
  0.0 287.1 jit_solution(8467454233105034597)
XLA Ops:
  6.5 1.4 maximum_bitcast_fusion
  7.9 3.6 %collective-permute-start.1 = (bf16[2,1,1,384,768]{4,3,0,2,1:T(8,128)(2,1)S(1)}, bf16[2,1,1,384,768]{4,3,0,2,1:T(8,128)(2,1)S(1)}, u32[]{:S(2)}, u32[]{:S(2)}) collective-permute-start(bf16[2,1,1,384,768]{4,3,0,2,1:T(8,128)(2,1)S(1)} %maximum_bitcast_fusion), channel_id=1, source_target_pairs={{32,0},{64,32},{96,64},{128,96},{160,128},{192,160},{224,192},{256... | collective-permute-start | bytes 3538952 | tf_op jit(solution)/shard_map/ppermute | solution.py:20
  11.5 1.9 collective-permute-start
  13.5 11.8 %collective-permute-done.1 = bf16[2,1,1,384,768]{4,3,0,2,1:T(8,128)(2,1)S(1)} collective-permute-done((bf16[2,1,1,384,768]{4,3,0,2,1:T(8,128)(2,1)S(1)}, bf16[2,1,1,384,768]{4,3,0,2,1:T(8,128)(2,1)S(1)}, u32[]{:S(2)}, u32[]{:S(2)}) %collective-permute-start.1) | collective-permute-done | bytes 1179680 | tf_op jit(solution)/shard_map/ppermute | solution.py:20
  25.3 6.3 %collective-permute-done = bf16[2,1,1,384,768]{4,3,0,2,1:T(8,128)(2,1)S(1)} collective-permute-done((bf16[2,1,1,384,768]{4,3,0,2,1:T(8,128)(2,1)S(1)}, bf16[2,1,1,384,768]{4,3,0,2,1:T(8,128)(2,1)S(1)}, u32[]{:S(2)}, u32[]{:S(2)}) %collective-permute-start) | collective-permute-done | bytes 1179680 | tf_op jit(solution)/shard_map/ppermute | solution.py:18
  31.6 1.9 pad_maximum_fusion.1
  33.5 1.3 collective-permute-start.3
  34.8 6.3 %collective-permute-start.2 = (bf16[2,3,1,384,768]{4,3,0,2,1:T(8,128)(2,1)}, bf16[2,3,1,384,768]{4,3,0,2,1:T(8,128)(2,1)}, u32[]{:S(2)}, u32[]{:S(2)}) collective-permute-start(bf16[2,3,1,384,768]{4,3,0,2,1:T(8,128)(2,1)} %pad_maximum_fusion.1), channel_id=1, source_target_pairs={{0,2},{2,4},{4,6},{6,8},{8,10},{10,12},{12,14},{14,16},{16,18},{18... | collective-permute-start | bytes 10616840 | tf_op jit(solution)/shard_map/ppermute | solution.py:18
  43.0 65.0 %collective-permute-done.3 = bf16[2,3,1,384,768]{4,3,0,2,1:T(8,128)(2,1)} collective-permute-done((bf16[2,3,1,384,768]{4,3,0,2,1:T(8,128)(2,1)}, bf16[2,3,1,384,768]{4,3,0,2,1:T(8,128)(2,1)}, u32[]{:S(2)}, u32[]{:S(2)}) %collective-permute-start.3) | collective-permute-done | bytes 3538976 | tf_op jit(solution)/shard_map/ppermute | solution.py:20
  108.0 1.7 collective-permute-done.2
  109.7 8.2 %pad_maximum_fusion = bf16[2,3,3,384,768]{4,3,0,2,1:T(8,128)(2,1)} fusion(bf16[2,3,1,384,768]{4,3,0,2,1:T(8,128)(2,1)} %collective-permute-done.3, bf16[2,1,1,384,768]{4,3,0,2,1:T(8,128)(2,1)S(1)} %collective-permute-done.1, bf16[2,1,1,384,768]{4,3,0,2,1:T(8,128)(2,1)S(1)} %maximum_bitcast_fusion, bf16[2,1,1,384,768]{4,3,0,2,1:T(8,128)(2,1)S(1)} %collective-permute-done, ...), kind=kLoop, calls=%fused_computation | loop fusion | flops 21233664 | bytes 21233664 | tf_op jit(solution)/shard_map/concatenate | solution.py:16
  117.9 8.9 %fusion.42 = (bf16[1,3,3,384,768]{4,3,0,2,1:T(8,128)(2,1)}, bf16[1,3,3,384,768]{4,3,0,2,1:T(8,128)(2,1)}) fusion(bf16[2,3,3,384,768]{4,3,0,2,1:T(8,128)(2,1)} %pad_maximum_fusion), kind=kLoop, calls=%fused_computation.77 | loop fusion | bytes 21233664 | tf_op jit(solution)/shard_map/slice | solution.py:45
  126.8 3.2 %fusion.43 = (f32[384]{0:T(512)S(1)}, f32[3456,384]{1,0:T(8,128)S(1)}) fusion(f32[3456]{0:T(1024)S(1)} %select_n.17, bf16[384,768]{1,0:T(8,128)(2,1)S(1)} %bitcast.31, bf16[3456,768]{1,0:T(8,128)(2,1)} %bitcast.23), kind=kOutput, calls=%fused_computation.78 | convolution fusion | flops 343719552 | bytes 6309376 | tf_op jit(solution)/shard_map/dot_general | solution.py:54
  130.1 1.1 fusion.44
  131.1 1.0 fusion.45
  132.2 1.1 fusion.46
  133.2 1.1 fusion.47
  134.3 1.1 fusion.48
  139.8 1.0 fusion.14
  141.6 1.0 fusion.16
  142.6 1.1 convert_reduce_fusion.1
  148.0 42.3 %all-gather.3.cloned.1.call-done = bf16[384,1536]{1,0:T(8,128)(2,1)} async-done(((bf16[384,768]{1,0:T(8,128)(2,1)}), bf16[384,1536]{1,0:T(8,128)(2,1)}) %all-gather.3.cloned.1.call-update) | async-done | bytes 1179664 | tf_op jit(solution)/shard_map/all_gather | solution.py:87
  190.4 84.1 %all-gather.5.cloned.1.call-done = bf16[1536,1536]{1,0:T(8,128)(2,1)} async-done(((bf16[96,1536]{1,0:T(8,128)(2,1)}), bf16[1536,1536]{1,0:T(8,128)(2,1)}) %all-gather.5.cloned.1.call-update) | async-done | bytes 4718608 | tf_op jit(solution)/shard_map/all_gather | solution.py:88
  274.5 5.7 %fusion.8 = bf16[1,1,384,1536]{3,2,1,0:T(8,128)(2,1)} fusion(bf16[384,1536]{1,0:T(8,128)(2,1)} %all-gather.3.cloned.1.call-done, bf16[1536,1536]{1,0:T(8,128)(2,1)} %all-gather.5.cloned.1.call-done, bf16[1,1,384,1536]{3,2,1,0:T(8,128)(2,1)S(1)} %copy-done.4, f32[1536]{0:T(1024)S(1)} %copy-done.5), kind=kOutput, calls=%fused_computation.29 | convolution fusion | flops 1814298624 | bytes 8263680 | tf_op jit(solution)/shard_map/dot_general | solution.py:89
  (39 shorter events, 11.5 us)
Async XLA Ops:
  6.5 34.6 %copy-start.3 = (s32[1,1,9]{2,1,0:T(1,128)S(1)}, s32[1,1,9]{2,1,0:T(1,128)}, u32[]{:S(2)}) copy-start(s32[1,1,9]{2,1,0:T(1,128)} %param.13) | copy-start | bytes 112
  6.5 183.8 %all-gather.3.cloned.1.call-start = ((), (), s32[]{:S(2)}) async-start(), calls=%async_computation | async-start | bytes 1769472 | tf_op jit(solution)/shard_map/all_gather | solution.py:87
  7.9 17.4 %collective-permute-start.1 = (bf16[2,1,1,384,768]{4,3,0,2,1:T(8,128)(2,1)S(1)}, bf16[2,1,1,384,768]{4,3,0,2,1:T(8,128)(2,1)S(1)}, u32[]{:S(2)}, u32[]{:S(2)}) collective-permute-start(bf16[2,1,1,384,768]{4,3,0,2,1:T(8,128)(2,1)S(1)} %maximum_bitcast_fusion), channel_id=1, source_target_pairs={{32,0},{64,32},{96,64},{128,96},{160,128},{192,160},{224,192},{256... | collective-permute-start | bytes 3538952 | tf_op jit(solution)/shard_map/ppermute | solution.py:20
  11.5 20.0 %collective-permute-start = (bf16[2,1,1,384,768]{4,3,0,2,1:T(8,128)(2,1)S(1)}, bf16[2,1,1,384,768]{4,3,0,2,1:T(8,128)(2,1)S(1)}, u32[]{:S(2)}, u32[]{:S(2)}) collective-permute-start(bf16[2,1,1,384,768]{4,3,0,2,1:T(8,128)(2,1)S(1)} %maximum_bitcast_fusion), channel_id=1, source_target_pairs={{0,32},{32,64},{64,96},{96,128},{128,160},{160,192},{192,224},{224... | collective-permute-start | bytes 3538952 | tf_op jit(solution)/shard_map/ppermute | solution.py:18
  33.5 74.5 %collective-permute-start.3 = (bf16[2,3,1,384,768]{4,3,0,2,1:T(8,128)(2,1)}, bf16[2,3,1,384,768]{4,3,0,2,1:T(8,128)(2,1)}, u32[]{:S(2)}, u32[]{:S(2)}) collective-permute-start(bf16[2,3,1,384,768]{4,3,0,2,1:T(8,128)(2,1)} %pad_maximum_fusion.1), channel_id=1, source_target_pairs={{2,0},{4,2},{6,4},{8,6},{10,8},{12,10},{14,12},{16,14},{18,16},{20... | collective-permute-start | bytes 10616840 | tf_op jit(solution)/shard_map/ppermute | solution.py:20
  34.8 74.9 %collective-permute-start.2 = (bf16[2,3,1,384,768]{4,3,0,2,1:T(8,128)(2,1)}, bf16[2,3,1,384,768]{4,3,0,2,1:T(8,128)(2,1)}, u32[]{:S(2)}, u32[]{:S(2)}) collective-permute-start(bf16[2,3,1,384,768]{4,3,0,2,1:T(8,128)(2,1)} %pad_maximum_fusion.1), channel_id=1, source_target_pairs={{0,2},{2,4},{4,6},{6,8},{8,10},{10,12},{12,14},{14,16},{16,18},{18... | collective-permute-start | bytes 10616840 | tf_op jit(solution)/shard_map/ppermute | solution.py:18
  117.9 8.9 %copy-start.2 = (bf16[1,1,384,768]{3,2,1,0:T(8,128)(2,1)S(1)}, bf16[1,1,384,768]{3,2,1,0:T(8,128)(2,1)}, u32[]{:S(2)}) copy-start(bf16[1,1,384,768]{3,2,1,0:T(8,128)(2,1)} %param.7) | copy-start | bytes 1769476
  126.8 3.3 %copy-start = (bf16[1,3,3,384,768]{4,3,0,2,1:T(8,128)(2,1)S(1)}, bf16[1,3,3,384,768]{4,3,0,2,1:T(8,128)(2,1)}, u32[]{:S(2)}) copy-start(bf16[1,3,3,384,768]{4,3,0,2,1:T(8,128)(2,1)} %get-tuple-element.5) | copy-start | bytes 15925252
  133.2 3.0 %slice-start = ((s8[5308416]{0:T(1024)(128)(4,1)}), s8[4194304]{0:T(1024)(128)(4,1)S(1)}, s32[]{:S(2)}) async-start(s8[5308416]{0:T(1024)(128)(4,1)} %bitcast.15), calls=%async_computation.2 | async-start | bytes 8388608
  134.3 1.9 slice-start.1
  145.5 129.0 %copy-start.4 = (bf16[1,1,384,1536]{3,2,1,0:T(8,128)(2,1)S(1)}, bf16[1,1,384,1536]{3,2,1,0:T(8,128)(2,1)}, u32[]{:S(2)}) copy-start(bf16[1,1,384,1536]{3,2,1,0:T(8,128)(2,1)} %param.10) | copy-start | bytes 3538948
  145.5 129.0 %copy-start.5 = (f32[1536]{0:T(1024)S(1)}, f32[1536]{0:T(1024)}, u32[]{:S(2)}) copy-start(f32[1536]{0:T(1024)} %param.11) | copy-start | bytes 18436
  146.4 0.8 copy-start.1
  147.3 127.2 %all-gather.5.cloned.1.call-start = ((), (), s32[]{:S(2)}) async-start(), calls=%async_computation.1 | async-start | bytes 5013504 | tf_op jit(solution)/shard_map/all_gather | solution.py:88
Sparse Core Ops, SparseCore 0:
  147.4 42.9 all-gather.2
  192.4 82.0 all-gather.4
where the time goes:
time: 287 us
  waiting for transfers between devices  212 us (74%)
  matrix products  20 us (7%)
  other arithmetic  17.2 us (6%)
  between operations  13.5 us (5%)
  starting transfers between devices  13.2 us (5%)
  local copies, waits for them, and re-layouts  11.3 us (4%)
    all_gather x1, waiting for transfers between devices, local(): full_weight = lax.all_gather(out_weight, 'height', axis=0, tiled=True)  84.1 us
    ppermute x2, waiting for transfers between devices, with_halo(): lax.ppermute(head, axis, [((i + 1) % count, i) for i in range(ends)])  76.8 us
    all_gather x1, waiting for transfers between devices, local(): gathered = lax.all_gather(attended, 'mp', axis=1, tiled=True)  42.3 us
    concatenate x2, other arithmetic, with_halo(): jnp.concatenate([lax.ppermute(tail, axis, [(i, (i + 1) % count) for i in...  10.1 us
    slice x1, local copies, waits for them, and re-layouts, dense_heads(): key_rows = beside_all[0].reshape(9 * tokens, -1)  8.92 us
    dot_general x6, matrix products, dense_heads(): lax.dot_general(query_rows[:, lower:upper], key_rows[:, lower:upper], (((...  8.54 us
    ppermute x2, starting transfers between devices, with_halo(): lax.ppermute(tail, axis, [(i, (i + 1) % count) for i in range(ends)])  8.22 us
    ppermute x2, waiting for transfers between devices, with_halo(): lax.ppermute(tail, axis, [(i, (i + 1) % count) for i in range(ends)])  8.02 us
  transfers between devices with their start and end apart: 6, of which 6 were waited for; matrix products, arithmetic and copies ran while one was open for 1% of the time, Pallas kernels for 0%

commit v1 on v0

--- a/solution.py
+++ b/solution.py
@@ -5,6 +5,12 @@
 from jax.sharding import PartitionSpec as P
 
 HD = 128
+
+
+def laid_out(blocks, dim):
+    dims = list(blocks.shape[1:])
+    dims[dim] *= blocks.shape[0]
+    return jnp.moveaxis(blocks, 0, dim).reshape(dims)
 
 
 def with_halo(cells, sides, width):
@@ -85,7 +91,19 @@
     chosen = slot_mask(tile_lists, frame_index, row_index, frame_count, row_count)
     attended = dense_heads(query_rows, beside_all, chosen, head_count)
     gathered = lax.all_gather(attended, "mp", axis=1, tiled=True)
-    full_weight = lax.all_gather(out_weight, "height", axis=0, tiled=True)
+    count_2 = lax.axis_size("height")
+    pairs = [(i_2, (i_2 + 1) % count_2) for i_2 in range(count_2)]
+    back = [(b, a) for a, b in pairs]
+    lower_2, upper_2 = ([], [])
+    for lap in range(count_2 - 1):
+        if lap % 2 == 0:
+            lower_2.append(lax.ppermute(lower_2[-1] if lower_2 else out_weight, "height", pairs))
+        else:
+            upper_2.append(lax.ppermute(upper_2[-1] if upper_2 else out_weight, "height", back))
+    tiles = jnp.stack([*lower_2[::-1], out_weight, *upper_2])
+    shift = lax.axis_index("height") - len(lower_2)
+    tiles = tiles[(jnp.arange(count_2) - shift) % count_2]
+    full_weight = laid_out(tiles, 0)
     mixed = jnp.dot(gathered, full_weight, preferred_element_type=jnp.float32)
     result = stream.reshape(tokens, -1).astype(jnp.float32) + gate_scale[None, :] * mixed
     return result.astype(jnp.bfloat16).reshape(stream.shape)

time: 287 us -> 265 us (0.923)
  the two profiles are of different devices: /device:TPU:10 before, /device:TPU:1 now
where the time goes in v1:
time: 265 us; the launch traced here: 264 us
  waiting for transfers between devices  112 us (42%)
  starting transfers between devices  64.9 us (24%)
  local copies, waits for them, and re-layouts  39.2 us (15%)
  matrix products  20 us (8%)
  between operations  13.8 us (5%)
  other arithmetic  13.7 us (5%)
    ppermute x2, waiting for transfers between devices, with_halo(): lax.ppermute(head, axis, [((i + 1) % count, i) for i in range(ends)])  54.3 us
    ppermute x7, starting transfers between devices, local(): lax.ppermute(upper_2[-1] if upper_2 else out_weight, 'height', back)  31.9 us
    all_gather x1, waiting for transfers between devices, local(): gathered = lax.all_gather(attended, 'mp', axis=1, tiled=True)  25.6 us
    ppermute x8, waiting for transfers between devices, local(): lax.ppermute(lower_2[-1] if lower_2 else out_weight, 'height', pairs)  21.7 us
    unnamed x47, local copies, waits for them, and re-layouts  21.5 us
    ppermute x8, starting transfers between devices, local(): lax.ppermute(lower_2[-1] if lower_2 else out_weight, 'height', pairs)  17.8 us
    ppermute x7, waiting for transfers between devices, local(): lax.ppermute(upper_2[-1] if upper_2 else out_weight, 'height', back)  9.45 us
    slice x1, local copies, waits for them, and re-layouts, dense_heads(): key_rows = beside_all[0].reshape(9 * tokens, -1)  8.95 us
  transfers between devices with their start and end apart: 20, of which 10 were waited for; matrix products, arithmetic and copies ran while one was open for 25% of the time, Pallas kernels for 0%

profile of v1, /device:TPU:1, one launch (start us, length us, event | category | flops | bytes accessed | tf_op | source)
XLA Modules:
  0.0 263.7 jit_solution(1291239974521514458)
XLA Ops:
  6.5 4.4 %collective-permute-start.4 = (bf16[96,1536]{1,0:T(8,128)(2,1)}, bf16[96,1536]{1,0:T(8,128)(2,1)S(1)}, u32[]{:S(2)}, u32[]{:S(2)}) collective-permute-start(bf16[96,1536]{1,0:T(8,128)(2,1)} %param.12), channel_id=1, source_target_pairs={{0,2},{2,4},{4,6},{6,8},{8,10},{10,12},{12,14},{14,16},{16,18},{18... | collective-permute-start | bytes 884744 | tf_op jit(solution)/shard_map/ppermute | solution.py:100
  10.9 14.5 %collective-permute-done.4 = bf16[96,1536]{1,0:T(8,128)(2,1)S(1)} collective-permute-done((bf16[96,1536]{1,0:T(8,128)(2,1)}, bf16[96,1536]{1,0:T(8,128)(2,1)S(1)}, u32[]{:S(2)}, u32[]{:S(2)}) %collective-permute-start.4) | collective-permute-done | bytes 294944 | tf_op jit(solution)/shard_map/ppermute | solution.py:100
  27.3 4.6 %collective-permute-start.12 = (bf16[96,1536]{1,0:T(8,128)(2,1)}, bf16[96,1536]{1,0:T(8,128)(2,1)}, u32[]{:S(2)}, u32[]{:S(2)}) collective-permute-start(bf16[96,1536]{1,0:T(8,128)(2,1)} %param.12), channel_id=1, source_target_pairs={{2,0},{4,2},{6,4},{8,6},{10,8},{12,10},{14,12},{16,14},{18,16},{20... | collective-permute-start | bytes 884744 | tf_op jit(solution)/shard_map/ppermute | solution.py:102
  31.9 3.9 %collective-permute-done.5 = bf16[96,1536]{1,0:T(8,128)(2,1)S(1)} collective-permute-done((bf16[96,1536]{1,0:T(8,128)(2,1)S(1)}, bf16[96,1536]{1,0:T(8,128)(2,1)S(1)}, u32[]{:S(2)}, u32[]{:S(2)}) %collective-permute-start.5) | collective-permute-done | bytes 294944 | tf_op jit(solution)/shard_map/ppermute | solution.py:100
  37.7 4.6 %collective-permute-start.13 = (bf16[96,1536]{1,0:T(8,128)(2,1)}, bf16[96,1536]{1,0:T(8,128)(2,1)}, u32[]{:S(2)}, u32[]{:S(2)}) collective-permute-start(bf16[96,1536]{1,0:T(8,128)(2,1)} %collective-permute-done.12), channel_id=1, source_target_pairs={{2,0},{4,2},{6,4},{8,6},{10,8},{12,10},{14,12},{16,14},{18,16},{20... | collective-permute-start | bytes 884744 | tf_op jit(solution)/shard_map/ppermute | solution.py:102
  42.3 3.0 %collective-permute-done.6 = bf16[96,1536]{1,0:T(8,128)(2,1)} collective-permute-done((bf16[96,1536]{1,0:T(8,128)(2,1)S(1)}, bf16[96,1536]{1,0:T(8,128)(2,1)}, u32[]{:S(2)}, u32[]{:S(2)}) %collective-permute-start.6) | collective-permute-done | bytes 294944 | tf_op jit(solution)/shard_map/ppermute | solution.py:100
  48.6 5.0 %collective-permute-start.1 = (bf16[2,1,1,384,768]{4,3,0,2,1:T(8,128)(2,1)S(1)}, bf16[2,1,1,384,768]{4,3,0,2,1:T(8,128)(2,1)S(1)}, u32[]{:S(2)}, u32[]{:S(2)}) collective-permute-start(bf16[2,1,1,384,768]{4,3,0,2,1:T(8,128)(2,1)S(1)} %maximum_bitcast_fusion), channel_id=1, source_target_pairs={{32,0},{64,32},{96,64},{128,96},{160,128},{192,160},{224,192},{256... | collective-permute-start | bytes 3538952 | tf_op jit(solution)/shard_map/ppermute | solution.py:26
  53.6 4.7 %collective-permute-start = (bf16[2,1,1,384,768]{4,3,0,2,1:T(8,128)(2,1)S(1)}, bf16[2,1,1,384,768]{4,3,0,2,1:T(8,128)(2,1)S(1)}, u32[]{:S(2)}, u32[]{:S(2)}) collective-permute-start(bf16[2,1,1,384,768]{4,3,0,2,1:T(8,128)(2,1)S(1)} %maximum_bitcast_fusion), channel_id=1, source_target_pairs={{0,32},{32,64},{64,96},{96,128},{128,160},{160,192},{192,224},{224... | collective-permute-start | bytes 3538952 | tf_op jit(solution)/shard_map/ppermute | solution.py:24
  58.4 4.9 %collective-permute-start.14 = (bf16[96,1536]{1,0:T(8,128)(2,1)}, bf16[96,1536]{1,0:T(8,128)(2,1)S(1)}, u32[]{:S(2)}, u32[]{:S(2)}) collective-permute-start(bf16[96,1536]{1,0:T(8,128)(2,1)} %collective-permute-done.13), channel_id=1, source_target_pairs={{2,0},{4,2},{6,4},{8,6},{10,8},{12,10},{14,12},{16,14},{18,16},{20... | collective-permute-start | bytes 884744 | tf_op jit(solution)/shard_map/ppermute | solution.py:102
  65.2 3.4 %collective-permute-done.14 = bf16[96,1536]{1,0:T(8,128)(2,1)S(1)} collective-permute-done((bf16[96,1536]{1,0:T(8,128)(2,1)}, bf16[96,1536]{1,0:T(8,128)(2,1)S(1)}, u32[]{:S(2)}, u32[]{:S(2)}) %collective-permute-start.14) | collective-permute-done | bytes 294944 | tf_op jit(solution)/shard_map/ppermute | solution.py:102
  69.3 4.9 %collective-permute-start.15 = (bf16[96,1536]{1,0:T(8,128)(2,1)S(1)}, bf16[96,1536]{1,0:T(8,128)(2,1)}, u32[]{:S(2)}, u32[]{:S(2)}) collective-permute-start(bf16[96,1536]{1,0:T(8,128)(2,1)S(1)} %collective-permute-done.14), channel_id=1, source_target_pairs={{2,0},{4,2},{6,4},{8,6},{10,8},{12,10},{14,12},{16,14},{18,16},{20... | collective-permute-start | bytes 884744 | tf_op jit(solution)/shard_map/ppermute | solution.py:102
  77.1 3.2 %collective-permute-done.15 = bf16[96,1536]{1,0:T(8,128)(2,1)} collective-permute-done((bf16[96,1536]{1,0:T(8,128)(2,1)S(1)}, bf16[96,1536]{1,0:T(8,128)(2,1)}, u32[]{:S(2)}, u32[]{:S(2)}) %collective-permute-start.15) | collective-permute-done | bytes 294944 | tf_op jit(solution)/shard_map/ppermute | solution.py:102
  80.3 5.1 %collective-permute-start.16 = (bf16[96,1536]{1,0:T(8,128)(2,1)}, bf16[96,1536]{1,0:T(8,128)(2,1)}, u32[]{:S(2)}, u32[]{:S(2)}) collective-permute-start(bf16[96,1536]{1,0:T(8,128)(2,1)} %collective-permute-done.15), channel_id=1, source_target_pairs={{2,0},{4,2},{6,4},{8,6},{10,8},{12,10},{14,12},{16,14},{18,16},{20... | collective-permute-start | bytes 884744 | tf_op jit(solution)/shard_map/ppermute | solution.py:102
  89.3 2.9 %collective-permute-done.16 = bf16[96,1536]{1,0:T(8,128)(2,1)} collective-permute-done((bf16[96,1536]{1,0:T(8,128)(2,1)}, bf16[96,1536]{1,0:T(8,128)(2,1)}, u32[]{:S(2)}, u32[]{:S(2)}) %collective-permute-start.16) | collective-permute-done | bytes 294944 | tf_op jit(solution)/shard_map/ppermute | solution.py:102
  92.1 5.3 %collective-permute-start.17 = (bf16[96,1536]{1,0:T(8,128)(2,1)}, bf16[96,1536]{1,0:T(8,128)(2,1)}, u32[]{:S(2)}, u32[]{:S(2)}) collective-permute-start(bf16[96,1536]{1,0:T(8,128)(2,1)} %collective-permute-done.16), channel_id=1, source_target_pairs={{2,0},{4,2},{6,4},{8,6},{10,8},{12,10},{14,12},{16,14},{18,16},{20... | collective-permute-start | bytes 884744 | tf_op jit(solution)/shard_map/ppermute | solution.py:102
  101.8 4.2 %collective-permute-start.2 = (bf16[2,3,1,384,768]{4,3,0,2,1:T(8,128)(2,1)S(1)}, bf16[2,3,1,384,768]{4,3,0,2,1:T(8,128)(2,1)S(1)}, u32[]{:S(2)}, u32[]{:S(2)}) collective-permute-start(bf16[2,3,1,384,768]{4,3,0,2,1:T(8,128)(2,1)S(1)} %pad_maximum_fusion.1), channel_id=1, source_target_pairs={{0,2},{2,4},{4,6},{6,8},{8,10},{10,12},{12,14},{14,16},{16,18},{18... | collective-permute-start | bytes 10616840 | tf_op jit(solution)/shard_map/ppermute | solution.py:24
  106.0 2.6 collective-permute-start.18
  125.0 54.3 %collective-permute-done.3 = bf16[2,3,1,384,768]{4,3,0,2,1:T(8,128)(2,1)S(1)} collective-permute-done((bf16[2,3,1,384,768]{4,3,0,2,1:T(8,128)(2,1)S(1)}, bf16[2,3,1,384,768]{4,3,0,2,1:T(8,128)(2,1)S(1)}, u32[]{:S(2)}, u32[]{:S(2)}) %collective-permute-start.3) | collective-permute-done | bytes 3538976 | tf_op jit(solution)/shard_map/ppermute | solution.py:26
  180.5 4.9 %pad_maximum_fusion = bf16[2,3,3,384,768]{4,3,0,2,1:T(8,128)(2,1)} fusion(bf16[2,3,1,384,768]{4,3,0,2,1:T(8,128)(2,1)S(1)} %collective-permute-done.3, bf16[2,1,1,384,768]{4,3,0,2,1:T(8,128)(2,1)S(1)} %collective-permute-done.1, bf16[2,1,1,384,768]{4,3,0,2,1:T(8,128)(2,1)S(1)} %maximum_bitcast_fusion, ...), kind=kLoop, calls=%fused_computation.1 | loop fusion | flops 21233664 | bytes 21233664 | tf_op jit(solution)/shard_map/concatenate | solution.py:22
  185.4 8.9 %fusion.44 = (bf16[1,3,3,384,768]{4,3,0,2,1:T(8,128)(2,1)}, bf16[1,3,3,384,768]{4,3,0,2,1:T(8,128)(2,1)}) fusion(bf16[2,3,3,384,768]{4,3,0,2,1:T(8,128)(2,1)} %pad_maximum_fusion), kind=kLoop, calls=%fused_computation.101 | loop fusion | bytes 21233664 | tf_op jit(solution)/shard_map/slice | solution.py:51
  194.4 3.2 %fusion.45 = (f32[384]{0:T(512)S(1)}, f32[3456,384]{1,0:T(8,128)S(1)}) fusion(f32[3456]{0:T(1024)S(1)} %select_n.41, bf16[384,768]{1,0:T(8,128)(2,1)S(1)} %bitcast.67, bf16[3456,768]{1,0:T(8,128)(2,1)} %bitcast.58), kind=kOutput, calls=%fused_computation.102 | convolution fusion | flops 343719552 | bytes 6309376 | tf_op jit(solution)/shard_map/dot_general | solution.py:60
  220.1 5.4 %gather_fusion = bf16[16,96,1536]{2,1,0:T(8,128)(2,1)} fusion(bf16[16,96,1536]{2,1,0:T(8,128)(2,1)} %bitcast_dynamic-update-slice_fusion, s32[1024]{0:T(1024)} %pad_clamp_fusion), kind=kCustom, calls=%fused_computation | custom fusion | bytes 9437248 | tf_op jit(solution)/shard_map/gather | solution.py:105
  225.5 25.6 %all-gather.2.cloned.1.call-done = bf16[384,1536]{1,0:T(8,128)(2,1)} async-done(((bf16[384,768]{1,0:T(8,128)(2,1)}), bf16[384,1536]{1,0:T(8,128)(2,1)}) %all-gather.2.cloned.1.call-update) | async-done | bytes 1179664 | tf_op jit(solution)/shard_map/all_gather | solution.py:93
  251.1 5.7 %fusion.8 = bf16[1,1,384,1536]{3,2,1,0:T(8,128)(2,1)} fusion(bf16[384,1536]{1,0:T(8,128)(2,1)} %all-gather.2.cloned.1.call-done, bf16[1536,1536]{1,0:T(8,128)(2,1)} %bitcast.64, bf16[1,1,384,1536]{3,2,1,0:T(8,128)(2,1)S(1)} %copy-done.12, f32[1536]{0:T(1024)S(1)} %copy-done.13), kind=kOutput, calls=%fused_computation.30 | convolution fusion | flops 1814298624 | bytes 8263680 | tf_op jit(solution)/shard_map/dot_general | solution.py:107
  (101 shorter events, 60.8 us)
Async XLA Ops:
  6.5 244.6 %all-gather.2.cloned.1.call-start = ((), (), s32[]{:S(2)}) async-start(), calls=%async_computation | async-start | bytes 1769472 | tf_op jit(solution)/shard_map/all_gather | solution.py:93
  6.5 18.9 %collective-permute-start.4 = (bf16[96,1536]{1,0:T(8,128)(2,1)}, bf16[96,1536]{1,0:T(8,128)(2,1)S(1)}, u32[]{:S(2)}, u32[]{:S(2)}) collective-permute-start(bf16[96,1536]{1,0:T(8,128)(2,1)} %param.12), channel_id=1, source_target_pairs={{0,2},{2,4},{4,6},{6,8},{8,10},{10,12},{12,14},{14,16},{16,18},{18... | collective-permute-start | bytes 884744 | tf_op jit(solution)/shard_map/ppermute | solution.py:100
  25.4 10.4 %collective-permute-start.5 = (bf16[96,1536]{1,0:T(8,128)(2,1)S(1)}, bf16[96,1536]{1,0:T(8,128)(2,1)S(1)}, u32[]{:S(2)}, u32[]{:S(2)}) collective-permute-start(bf16[96,1536]{1,0:T(8,128)(2,1)S(1)} %collective-permute-done.4), channel_id=1, source_target_pairs={{0,2},{2,4},{4,6},{6,8},{8,10},{10,12},{12,14},{14,16},{16,18},{18... | collective-permute-start | bytes 884744 | tf_op jit(solution)/shard_map/ppermute | solution.py:100
  27.3 10.4 %collective-permute-start.12 = (bf16[96,1536]{1,0:T(8,128)(2,1)}, bf16[96,1536]{1,0:T(8,128)(2,1)}, u32[]{:S(2)}, u32[]{:S(2)}) collective-permute-start(bf16[96,1536]{1,0:T(8,128)(2,1)} %param.12), channel_id=1, source_target_pairs={{2,0},{4,2},{6,4},{8,6},{10,8},{12,10},{14,12},{16,14},{18,16},{20... | collective-permute-start | bytes 884744 | tf_op jit(solution)/shard_map/ppermute | solution.py:102
  35.8 9.6 %collective-permute-start.6 = (bf16[96,1536]{1,0:T(8,128)(2,1)S(1)}, bf16[96,1536]{1,0:T(8,128)(2,1)}, u32[]{:S(2)}, u32[]{:S(2)}) collective-permute-start(bf16[96,1536]{1,0:T(8,128)(2,1)S(1)} %collective-permute-done.5), channel_id=1, source_target_pairs={{0,2},{2,4},{4,6},{6,8},{8,10},{10,12},{12,14},{14,16},{16,18},{18... | collective-permute-start | bytes 884744 | tf_op jit(solution)/shard_map/ppermute | solution.py:100
  37.7 20.6 %collective-permute-start.13 = (bf16[96,1536]{1,0:T(8,128)(2,1)}, bf16[96,1536]{1,0:T(8,128)(2,1)}, u32[]{:S(2)}, u32[]{:S(2)}) collective-permute-start(bf16[96,1536]{1,0:T(8,128)(2,1)} %collective-permute-done.12), channel_id=1, source_target_pairs={{2,0},{4,2},{6,4},{8,6},{10,8},{12,10},{14,12},{16,14},{18,16},{20... | collective-permute-start | bytes 884744 | tf_op jit(solution)/shard_map/ppermute | solution.py:102
  45.3 17.9 %collective-permute-start.7 = (bf16[96,1536]{1,0:T(8,128)(2,1)}, bf16[96,1536]{1,0:T(8,128)(2,1)}, u32[]{:S(2)}, u32[]{:S(2)}) collective-permute-start(bf16[96,1536]{1,0:T(8,128)(2,1)} %collective-permute-done.6), channel_id=1, source_target_pairs={{0,2},{2,4},{4,6},{6,8},{8,10},{10,12},{12,14},{14,16},{16,18},{18... | collective-permute-start | bytes 884744 | tf_op jit(solution)/shard_map/ppermute | solution.py:100
  48.6 51.4 %collective-permute-start.1 = (bf16[2,1,1,384,768]{4,3,0,2,1:T(8,128)(2,1)S(1)}, bf16[2,1,1,384,768]{4,3,0,2,1:T(8,128)(2,1)S(1)}, u32[]{:S(2)}, u32[]{:S(2)}) collective-permute-start(bf16[2,1,1,384,768]{4,3,0,2,1:T(8,128)(2,1)S(1)} %maximum_bitcast_fusion), channel_id=1, source_target_pairs={{32,0},{64,32},{96,64},{128,96},{160,128},{192,160},{224,192},{256... | collective-permute-start | bytes 3538952 | tf_op jit(solution)/shard_map/ppermute | solution.py:26
  53.6 46.4 %collective-permute-start = (bf16[2,1,1,384,768]{4,3,0,2,1:T(8,128)(2,1)S(1)}, bf16[2,1,1,384,768]{4,3,0,2,1:T(8,128)(2,1)S(1)}, u32[]{:S(2)}, u32[]{:S(2)}) collective-permute-start(bf16[2,1,1,384,768]{4,3,0,2,1:T(8,128)(2,1)S(1)} %maximum_bitcast_fusion), channel_id=1, source_target_pairs={{0,32},{32,64},{64,96},{96,128},{128,160},{160,192},{192,224},{224... | collective-permute-start | bytes 3538952 | tf_op jit(solution)/shard_map/ppermute | solution.py:24
  58.4 10.2 %collective-permute-start.14 = (bf16[96,1536]{1,0:T(8,128)(2,1)}, bf16[96,1536]{1,0:T(8,128)(2,1)S(1)}, u32[]{:S(2)}, u32[]{:S(2)}) collective-permute-start(bf16[96,1536]{1,0:T(8,128)(2,1)} %collective-permute-done.13), channel_id=1, source_target_pairs={{2,0},{4,2},{6,4},{8,6},{10,8},{12,10},{14,12},{16,14},{18,16},{20... | collective-permute-start | bytes 884744 | tf_op jit(solution)/shard_map/ppermute | solution.py:102
  63.2 11.0 %collective-permute-start.8 = (bf16[96,1536]{1,0:T(8,128)(2,1)}, bf16[96,1536]{1,0:T(8,128)(2,1)S(1)}, u32[]{:S(2)}, u32[]{:S(2)}) collective-permute-start(bf16[96,1536]{1,0:T(8,128)(2,1)} %collective-permute-done.7), channel_id=1, source_target_pairs={{0,2},{2,4},{4,6},{6,8},{8,10},{10,12},{12,14},{14,16},{16,18},{18... | collective-permute-start | bytes 884744 | tf_op jit(solution)/shard_map/ppermute | solution.py:100
  69.3 11.0 %collective-permute-start.15 = (bf16[96,1536]{1,0:T(8,128)(2,1)S(1)}, bf16[96,1536]{1,0:T(8,128)(2,1)}, u32[]{:S(2)}, u32[]{:S(2)}) collective-permute-start(bf16[96,1536]{1,0:T(8,128)(2,1)S(1)} %collective-permute-done.14), channel_id=1, source_target_pairs={{2,0},{4,2},{6,4},{8,6},{10,8},{12,10},{14,12},{16,14},{18,16},{20... | collective-permute-start | bytes 884744 | tf_op jit(solution)/shard_map/ppermute | solution.py:102
  74.2 11.5 %collective-permute-start.9 = (bf16[96,1536]{1,0:T(8,128)(2,1)S(1)}, bf16[96,1536]{1,0:T(8,128)(2,1)}, u32[]{:S(2)}, u32[]{:S(2)}) collective-permute-start(bf16[96,1536]{1,0:T(8,128)(2,1)S(1)} %collective-permute-done.8), channel_id=1, source_target_pairs={{0,2},{2,4},{4,6},{6,8},{8,10},{10,12},{12,14},{14,16},{16,18},{18... | collective-permute-start | bytes 884744 | tf_op jit(solution)/shard_map/ppermute | solution.py:100
  80.3 11.8 %collective-permute-start.16 = (bf16[96,1536]{1,0:T(8,128)(2,1)}, bf16[96,1536]{1,0:T(8,128)(2,1)}, u32[]{:S(2)}, u32[]{:S(2)}) collective-permute-start(bf16[96,1536]{1,0:T(8,128)(2,1)} %collective-permute-done.15), channel_id=1, source_target_pairs={{2,0},{4,2},{6,4},{8,6},{10,8},{12,10},{14,12},{16,14},{18,16},{20... | collective-permute-start | bytes 884744 | tf_op jit(solution)/shard_map/ppermute | solution.py:102
  85.8 11.7 %collective-permute-start.10 = (bf16[96,1536]{1,0:T(8,128)(2,1)}, bf16[96,1536]{1,0:T(8,128)(2,1)}, u32[]{:S(2)}, u32[]{:S(2)}) collective-permute-start(bf16[96,1536]{1,0:T(8,128)(2,1)} %collective-permute-done.9), channel_id=1, source_target_pairs={{0,2},{2,4},{4,6},{6,8},{8,10},{10,12},{12,14},{14,16},{16,18},{18... | collective-permute-start | bytes 884744 | tf_op jit(solution)/shard_map/ppermute | solution.py:100
  89.3 23.5 %copy-start.11 = (bf16[96,1536]{1,0:T(8,128)(2,1)S(1)}, bf16[96,1536]{1,0:T(8,128)(2,1)}, u32[]{:S(2)}) copy-start(bf16[96,1536]{1,0:T(8,128)(2,1)} %copy-done.10) | copy-start | bytes 884740
  92.1 13.9 %collective-permute-start.17 = (bf16[96,1536]{1,0:T(8,128)(2,1)}, bf16[96,1536]{1,0:T(8,128)(2,1)}, u32[]{:S(2)}, u32[]{:S(2)}) collective-permute-start(bf16[96,1536]{1,0:T(8,128)(2,1)} %collective-permute-done.16), channel_id=1, source_target_pairs={{2,0},{4,2},{6,4},{8,6},{10,8},{12,10},{14,12},{16,14},{18,16},{20... | collective-permute-start | bytes 884744 | tf_op jit(solution)/shard_map/ppermute | solution.py:102
  97.5 11.1 %collective-permute-start.11 = (bf16[96,1536]{1,0:T(8,128)(2,1)}, bf16[96,1536]{1,0:T(8,128)(2,1)S(1)}, u32[]{:S(2)}, u32[]{:S(2)}) collective-permute-start(bf16[96,1536]{1,0:T(8,128)(2,1)} %collective-permute-done.10), channel_id=1, source_target_pairs={{0,2},{2,4},{4,6},{6,8},{8,10},{10,12},{12,14},{14,16},{16,18},{18... | collective-permute-start | bytes 884744 | tf_op jit(solution)/shard_map/ppermute | solution.py:100
  100.0 22.5 %copy-start.9 = (bf16[96,1536]{1,0:T(8,128)(2,1)S(1)}, bf16[96,1536]{1,0:T(8,128)(2,1)}, u32[]{:S(2)}) copy-start(bf16[96,1536]{1,0:T(8,128)(2,1)} %copy-done.8) | copy-start | bytes 884740
  100.5 78.8 %collective-permute-start.3 = (bf16[2,3,1,384,768]{4,3,0,2,1:T(8,128)(2,1)S(1)}, bf16[2,3,1,384,768]{4,3,0,2,1:T(8,128)(2,1)S(1)}, u32[]{:S(2)}, u32[]{:S(2)}) collective-permute-start(bf16[2,3,1,384,768]{4,3,0,2,1:T(8,128)(2,1)S(1)} %pad_maximum_fusion.1), channel_id=1, source_target_pairs={{2,0},{4,2},{6,4},{8,6},{10,8},{12,10},{14,12},{16,14},{18,16},{20... | collective-permute-start | bytes 10616840 | tf_op jit(solution)/shard_map/ppermute | solution.py:26
  101.8 78.7 %collective-permute-start.2 = (bf16[2,3,1,384,768]{4,3,0,2,1:T(8,128)(2,1)S(1)}, bf16[2,3,1,384,768]{4,3,0,2,1:T(8,128)(2,1)S(1)}, u32[]{:S(2)}, u32[]{:S(2)}) collective-permute-start(bf16[2,3,1,384,768]{4,3,0,2,1:T(8,128)(2,1)S(1)} %pad_maximum_fusion.1), channel_id=1, source_target_pairs={{0,2},{2,4},{4,6},{6,8},{8,10},{10,12},{12,14},{14,16},{16,18},{18... | collective-permute-start | bytes 10616840 | tf_op jit(solution)/shard_map/ppermute | solution.py:24
  106.0 112.3 %collective-permute-start.18 = (bf16[96,1536]{1,0:T(8,128)(2,1)}, bf16[96,1536]{1,0:T(8,128)(2,1)}, u32[]{:S(2)}, u32[]{:S(2)}) collective-permute-start(bf16[96,1536]{1,0:T(8,128)(2,1)} %collective-permute-done.17), channel_id=1, source_target_pairs={{2,0},{4,2},{6,4},{8,6},{10,8},{12,10},{14,12},{16,14},{18,16},{20... | collective-permute-start | bytes 884744 | tf_op jit(solution)/shard_map/ppermute | solution.py:102
  216.5 34.6 %copy-start.12 = (bf16[1,1,384,1536]{3,2,1,0:T(8,128)(2,1)S(1)}, bf16[1,1,384,1536]{3,2,1,0:T(8,128)(2,1)}, u32[]{:S(2)}) copy-start(bf16[1,1,384,1536]{3,2,1,0:T(8,128)(2,1)} %param.10) | copy-start | bytes 3538948
  216.5 34.6 %copy-start.13 = (f32[1536]{0:T(1024)S(1)}, f32[1536]{0:T(1024)}, u32[]{:S(2)}) copy-start(f32[1536]{0:T(1024)} %param.11) | copy-start | bytes 18436
  (12 other events, 111.1 us)
Sparse Core Ops, SparseCore 0:
  214.9 36.1 all-gather.1
